TPU v7x, 32 devices: a whole 2x2x4 slice. The times are simulated.
32 devices in a mesh: node: 4 (over y, x), local: 8 (over z, core).
Axes of the slice: x: 2, y: 2, z: 4, core: 2. Of those that a mesh axis runs over, the one named last changes fastest.
Arguments:
- tokens: bfloat16 [4096, 7168], P(('node', 'local')), may hold values from -6 to 6
- route_ids: int32 [4096, 8], P(('node', 'local')), may hold values from 0 to 383, all different within a row; in each aligned block of 128 rows (0 to 127, 128 to 255, ...) at most 5 rows name the same one
- route_gates: bfloat16 [4096, 8], P(('node', 'local')), may hold values from 0.099609375 to 1
- limits: int32 [384], replicated, may hold values from 1 to 5, as said below
- w_gate: bfloat16 [32, 7168, 448], P(('node', 'local')), may hold values from -0.0625 to 0.0625
- w_up: bfloat16 [32, 7168, 448], P(('node', 'local')), may hold values from -0.0625 to 0.0625
- w_down: bfloat16 [32, 448, 7168], P(('node', 'local')), may hold values from -0.125 to 0.125
Outputs:
- mixed: bfloat16 [4096, 7168], P(('node', 'local'))
Inputs may be any that keep to these rules, and one draw needn't show every extreme that they name: `route_ids`: in each aligned block of 128 rows (the rows of one device) no expert is named by more than 5 rows, a bound that some block reaches; a row names 8 different experts. `limits`: some expert's capacity is exactly 5.
All inputs are finite; a program needn't handle non-finite values.
Results may differ from a plain program's by a relative error of at most 0.0057.
Values may be sent and summed in bfloat16 or wider, within the bound.
A program may use at most 128 MiB of HBM per device.

v0:
```python
import jax
import jax.numpy as jnp
from jax import lax
from jax.sharding import PartitionSpec as P

GROUP = 4
CAP = 5


def slab_output(packed, gate_slab, up_slab, down_slab):
    flat_rows = packed.reshape(-1, packed.shape[-1])
    gate_act = jnp.dot(flat_rows, gate_slab, preferred_element_type=jnp.float32)
    upper = jnp.dot(flat_rows, up_slab, preferred_element_type=jnp.float32)
    hidden = (jax.nn.silu(gate_act) * upper).astype(jnp.bfloat16)
    result = jnp.dot(hidden, down_slab, preferred_element_type=jnp.float32).astype(jnp.bfloat16)
    return result.reshape(packed.shape[:-1] + (down_slab.shape[1],))


def routing(route_ids, route_gates, limits, hosted):
    experts = jnp.arange(hosted, dtype=jnp.int32)
    matches = route_ids[:, :, None] == experts[None, None, :]
    per_tok = jnp.sum(matches.astype(jnp.int32), axis=1)
    before = jnp.cumsum(per_tok, axis=0) - per_tok
    keep_mask = (per_tok > 0) & (before < limits[None, :hosted])
    gate_sum = jnp.sum(jnp.where(matches, route_gates.astype(jnp.float32)[:, :, None], 0.0), axis=1)
    return (keep_mask, before, jnp.where(keep_mask, gate_sum, 0.0))


def on_device(tokens, route_ids, route_gates, limits, w_gate, w_up, w_down):
    node_count = lax.axis_size("node")
    local_count = lax.axis_size("local")
    exp_node = local_count // GROUP
    hosted = node_count * exp_node
    tok_rows = tokens.shape[0]
    width = tokens.shape[1]
    keep_mask, before, weights = routing(route_ids, route_gates, limits, hosted)
    gate_slab, up_slab, down_slab = (w_gate[0], w_up[0], w_down[0])
    capacity = jnp.arange(CAP, dtype=jnp.int32)
    node_rows = min(tok_rows, exp_node * CAP)
    kept_nodes = keep_mask.reshape(tok_rows, node_count, exp_node)
    needed = jnp.any(kept_nodes, axis=2)
    needed_int = needed.astype(jnp.int32)
    position = jnp.cumsum(needed_int, axis=0) - needed_int
    slots = jnp.arange(node_rows, dtype=jnp.int32)
    placed = needed[:, :, None] & (position[:, :, None] == slots[None, None, :])
    rows_out = jnp.einsum(
        "tms,td->msd", placed.astype(jnp.bfloat16), tokens, preferred_element_type=jnp.float32
    ).astype(jnp.bfloat16)
    rank_tok = (jnp.where(keep_mask, before, -1) + 1).reshape(tok_rows, node_count, exp_node)
    ranks_out = jnp.einsum("tms,tmg->msg", placed.astype(jnp.int32), rank_tok) - 1
    gates_out = jnp.einsum(
        "tms,tmg->msg",
        placed.astype(jnp.float32),
        weights.reshape(tok_rows, node_count, exp_node),
        precision=lax.Precision.HIGHEST,
    ).astype(jnp.bfloat16)
    rows_in, gates_in, ranks_in = (
        lax.all_to_all(rows_out, "node", split_axis=0, concat_axis=0, tiled=True),
        lax.all_to_all(gates_out, "node", split_axis=0, concat_axis=0, tiled=True),
        lax.all_to_all(ranks_out, "node", split_axis=0, concat_axis=0, tiled=True),
    )
    matched = ranks_in[:, :, :, None] == capacity[None, None, None, :]
    forward = jnp.einsum(
        "nrgc,nrd->gncd", matched.astype(jnp.bfloat16), rows_in, preferred_element_type=jnp.float32
    ).astype(jnp.bfloat16)
    forward = jnp.broadcast_to(forward[:, None], (exp_node, GROUP, node_count, CAP, width)).reshape(
        local_count, node_count, CAP, width
    )
    returned = lax.all_to_all(
        slab_output(
            lax.all_to_all(forward, "local", split_axis=0, concat_axis=0, tiled=True),
            gate_slab,
            up_slab,
            down_slab,
        ),
        "local",
        split_axis=0,
        concat_axis=0,
        tiled=True,
    )
    summed = jnp.sum(
        returned.astype(jnp.float32).reshape(exp_node, GROUP, node_count, CAP, width), axis=1
    )
    combine = jnp.where(matched, gates_in.astype(jnp.float32)[:, :, :, None], 0.0)
    merged = jnp.einsum("nrgc,gncd->nrd", combine, summed, precision=lax.Precision.HIGHEST)
    gathered_back = lax.all_to_all(
        merged.astype(jnp.bfloat16), "node", split_axis=0, concat_axis=0, tiled=True
    ).astype(merged.dtype)
    mixed = jnp.einsum(
        "tms,msd->td", placed.astype(jnp.float32), gathered_back, precision=lax.Precision.HIGHEST
    )
    return mixed.astype(jnp.bfloat16)


def solution(mesh):
    return jax.shard_map(
        on_device,
        mesh=mesh,
        in_specs=(
            P(("node", "local"), None),
            P(("node", "local"), None),
            P(("node", "local"), None),
            P(),
            P(("node", "local"), None, None),
            P(("node", "local"), None, None),
            P(("node", "local"), None, None),
        ),
        out_specs=P(("node", "local"), None),
        check_vma=False,
    )
```

profile of v0, /device:TPU:24, one launch (start us, length us, event | category | flops | bytes accessed | tf_op | source)
XLA Modules:
  0.0 206.5 jit_solution(15980732791436523725)
XLA Ops:
  0.0 0.0 copy-start
  0.0 0.8 slice.9
  0.8 0.1 lt.13
  0.9 0.1 copy.81
  1.0 0.7 convert_element_type.53
  1.7 0.7 convert_reduce_fusion.1
  2.4 0.7 select_reduce_fusion
  3.1 0.2 copy.78
  3.3 0.1 fusion.47
  3.4 0.1 copy.79
  3.5 0.1 copy_select_fusion
  3.6 0.1 copy.82
  3.8 0.2 reduce_window_sum.23
  3.9 0.1 copy.84
  4.0 0.8 convolution_add_fusion
  4.8 3.7 %all-to-all-start = ((s32[4,10,2]{1,2,0:T(2,128)}), s32[4,10,2]{1,2,0:T(2,128)S(1)}, u32[]{:S(2)}, u32[]{:S(2)}) async-start(s32[4,10,2]{1,2,0:T(2,128)} %convolution_add_fusion), calls=%async_computation | async-start | bytes 8192 | tf_op jit(solution)/shard_map/all_to_all | solution.py:60
  8.5 0.0 copy-done
  8.5 0.4 convolution_convert_fusion.2
  8.9 4.3 %all-to-all-done = s32[4,10,2]{1,2,0:T(2,128)S(1)} async-done(((s32[4,10,2]{1,2,0:T(2,128)}), s32[4,10,2]{1,2,0:T(2,128)S(1)}, u32[]{:S(2)}, u32[]{:S(2)}) %all-to-all-start) | async-done | bytes 352 | tf_op jit(solution)/shard_map/all_to_all | solution.py:60
  13.2 14.0 %all_to_all.30 = bf16[4,10,7168]{2,1,0:T(8,128)(2,1)S(1)} all-to-all(bf16[4,10,7168]{2,1,0:T(8,128)(2,1)S(1)} %convolution_convert_fusion.2), channel_id=1, replica_groups=mesh['node'=4,'local'=8] {'node'}, dimensions={0} | all-to-all | bytes 1146880 | tf_op jit(solution)/shard_map/all_to_all | solution.py:58
  27.2 0.4 fusion.2
  27.5 0.5 copy.88
  28.1 2.0 broadcast_in_dim.54
  30.1 5.1 %all-to-all-start.3 = ((bf16[8,4,5,7168]{3,1,2,0:T(4,128)(2,1)}), bf16[8,4,5,7168]{3,1,2,0:T(4,128)(2,1)}, u32[]{:S(2)}, u32[]{:S(2)}) async-start(bf16[8,4,5,7168]{3,1,2,0:T(4,128)(2,1)} %bitcast.44), calls=%async_computation.3 | async-start | bytes 4587520 | tf_op jit(solution)/shard_map/all_to_all | solution.py:71
  35.2 0.7 convolution_convert_fusion.3
  35.9 50.1 %all-to-all-done.3 = bf16[8,4,5,7168]{3,1,2,0:T(4,128)(2,1)} async-done(((bf16[8,4,5,7168]{3,1,2,0:T(4,128)(2,1)}), bf16[8,4,5,7168]{3,1,2,0:T(4,128)(2,1)}, u32[]{:S(2)}, u32[]{:S(2)}) %all-to-all-start.3) | async-done | bytes 2293792 | tf_op jit(solution)/shard_map/all_to_all | solution.py:71
  86.0 3.2 %all-to-all-start.1 = ((bf16[4,10,2]{1,2,0:T(2,128)(2,1)}), bf16[4,10,2]{1,2,0:T(2,128)(2,1)S(1)}, u32[]{:S(2)}, u32[]{:S(2)}) async-start(bf16[4,10,2]{1,2,0:T(2,128)(2,1)} %convolution_convert_fusion.3), calls=%async_computation.1 | async-start | bytes 4096 | tf_op jit(solution)/shard_map/all_to_all | solution.py:59
  89.2 4.3 %copy.89 = bf16[8,4,5,7168]{3,2,1,0:T(8,128)(2,1)} copy(bf16[8,4,5,7168]{3,1,2,0:T(4,128)(2,1)} %all-to-all-done.3) | data formatting | bytes 4587520 | tf_op jit(solution)/shard_map/all_to_all | solution.py:71
  93.6 4.6 %reshape.65 = bf16[160,7168]{1,0:T(8,128)(2,1)} reshape(bf16[8,4,5,7168]{3,2,1,0:T(8,128)(2,1)} %copy.89) | data formatting | bytes 4587520 | tf_op jit(solution)/shard_map/reshape | solution.py:11
  98.2 5.5 %fusion.6 = f32[160,448]{1,0:T(8,128)S(1)} fusion(bf16[160,7168]{1,0:T(8,128)(2,1)} %reshape.65, bf16[1,7168,448]{1,2,0:T(8,128)(2,1)} %param.11), kind=kOutput, calls=%fused_computation.11 | convolution fusion | flops 1027604480 | bytes 9003008 | tf_op jit(solution)/shard_map/dot_general | solution.py:12
  103.7 10.4 %convolution_convert_fusion = bf16[160,7168]{1,0:T(8,128)(2,1)} fusion(bf16[1,448,7168]{2,1,0:T(8,128)(2,1)} %param.13, bf16[160,7168]{1,0:T(8,128)(2,1)} %reshape.65, bf16[1,7168,448]{1,2,0:T(8,128)(2,1)} %param.12, f32[160,448]{1,0:T(8,128)S(1)} %fusion.6), kind=kOutput, calls=%fused_computation.1 | convolution fusion | flops 2056785920 | bytes 17719296 | tf_op jit(solution)/shard_map/dot_general | solution.py:15
  114.2 4.6 %reshape.66 = bf16[8,4,5,7168]{3,2,1,0:T(8,128)(2,1)} reshape(bf16[160,7168]{1,0:T(8,128)(2,1)} %convolution_convert_fusion) | data formatting | bytes 4587520 | tf_op jit(solution)/shard_map/reshape | solution.py:16
  118.7 5.4 %copy.90 = bf16[8,4,5,7168]{3,1,2,0:T(4,128)(2,1)} copy(bf16[8,4,5,7168]{3,2,1,0:T(8,128)(2,1)} %reshape.66) | data formatting | bytes 4587520 | tf_op jit(solution)/shard_map/reshape | solution.py:16
  124.1 0.0 all-to-all-done.1
  124.1 6.8 %all-to-all-start.4 = ((bf16[8,4,5,7168]{3,1,2,0:T(4,128)(2,1)}), bf16[8,4,5,7168]{3,1,2,0:T(4,128)(2,1)}, u32[]{:S(2)}, u32[]{:S(2)}) async-start(bf16[8,4,5,7168]{3,1,2,0:T(4,128)(2,1)} %copy.90), calls=%async_computation.4 | async-start | bytes 4587520 | tf_op jit(solution)/shard_map/all_to_all | solution.py:69
  131.0 50.8 %all-to-all-done.4 = bf16[8,4,5,7168]{3,1,2,0:T(4,128)(2,1)} async-done(((bf16[8,4,5,7168]{3,1,2,0:T(4,128)(2,1)}), bf16[8,4,5,7168]{3,1,2,0:T(4,128)(2,1)}, u32[]{:S(2)}, u32[]{:S(2)}) %all-to-all-start.4) | async-done | bytes 2293792 | tf_op jit(solution)/shard_map/all_to_all | solution.py:69
  181.8 3.0 %convert_reduce_fusion = f32[2,4,5,7168]{3,1,2,0:T(4,128)S(1)} fusion(bf16[8,4,5,7168]{3,1,2,0:T(4,128)(2,1)} %all-to-all-done.4), kind=kLoop, calls=%fused_computation.13 | loop fusion | flops 2007040 | bytes 3440640 | tf_op jit(solution)/shard_map/reduce_sum | solution.py:81
  184.8 2.9 %fusion.1 = bf16[4,10,7168]{2,1,0:T(8,128)(2,1)S(1)} fusion(f32[2,4,5,7168]{3,1,2,0:T(4,128)S(1)} %convert_reduce_fusion, f32[4,10,2]{1,2,0:T(2,128)S(1)} %convert_element_type.55, s32[4,10,2]{1,2,0:T(2,128)S(1)} %all-to-all-done), kind=kOutput, calls=%fused_computation.4 | convolution fusion | flops 34693920 | bytes 1720960 | tf_op jit(solution)/shard_map/nrgc,gncd->nrd/dot_general | solution.py:85
  187.7 16.9 %all_to_all.31 = bf16[4,10,7168]{2,1,0:T(8,128)(2,1)S(1)} all-to-all(bf16[4,10,7168]{2,1,0:T(8,128)(2,1)S(1)} %fusion.1), channel_id=1, replica_groups=mesh['node'=4,'local'=8] {'node'}, dimensions={0} | all-to-all | bytes 1146880 | tf_op jit(solution)/shard_map/all_to_all | solution.py:86
  204.6 1.9 fusion
  (5 shorter events, 0.1 us)
Async XLA Ops:
  0.0 8.5 %copy-start = (bf16[128,7168]{1,0:T(8,128)(2,1)S(1)}, bf16[128,7168]{1,0:T(8,128)(2,1)}, u32[]{:S(2)}) copy-start(bf16[128,7168]{1,0:T(8,128)(2,1)} %param.7) | copy-start | bytes 5505028
  4.8 8.4 %all-to-all-start = ((s32[4,10,2]{1,2,0:T(2,128)}), s32[4,10,2]{1,2,0:T(2,128)S(1)}, u32[]{:S(2)}, u32[]{:S(2)}) async-start(s32[4,10,2]{1,2,0:T(2,128)} %convolution_add_fusion), calls=%async_computation | async-start | bytes 8192 | tf_op jit(solution)/shard_map/all_to_all | solution.py:60
  30.1 55.9 %all-to-all-start.3 = ((bf16[8,4,5,7168]{3,1,2,0:T(4,128)(2,1)}), bf16[8,4,5,7168]{3,1,2,0:T(4,128)(2,1)}, u32[]{:S(2)}, u32[]{:S(2)}) async-start(bf16[8,4,5,7168]{3,1,2,0:T(4,128)(2,1)} %bitcast.44), calls=%async_computation.3 | async-start | bytes 4587520 | tf_op jit(solution)/shard_map/all_to_all | solution.py:71
  86.0 38.1 %all-to-all-start.1 = ((bf16[4,10,2]{1,2,0:T(2,128)(2,1)}), bf16[4,10,2]{1,2,0:T(2,128)(2,1)S(1)}, u32[]{:S(2)}, u32[]{:S(2)}) async-start(bf16[4,10,2]{1,2,0:T(2,128)(2,1)} %convolution_convert_fusion.3), calls=%async_computation.1 | async-start | bytes 4096 | tf_op jit(solution)/shard_map/all_to_all | solution.py:59
  124.1 57.6 %all-to-all-start.4 = ((bf16[8,4,5,7168]{3,1,2,0:T(4,128)(2,1)}), bf16[8,4,5,7168]{3,1,2,0:T(4,128)(2,1)}, u32[]{:S(2)}, u32[]{:S(2)}) async-start(bf16[8,4,5,7168]{3,1,2,0:T(4,128)(2,1)} %copy.90), calls=%async_computation.4 | async-start | bytes 4587520 | tf_op jit(solution)/shard_map/all_to_all | solution.py:69
where the time goes:
time: 211 us; the launch traced here: 207 us
  waiting for transfers between devices  105 us (50%)
  blocking collectives  30.9 us (15%)
  matrix products  23 us (11%)
  local copies, waits for them, and re-layouts  22.9 us (11%)
  starting transfers between devices  18.9 us (9%)
  other arithmetic  5.55 us (3%)
    all_to_all x1, waiting for transfers between devices, on_device(): lax.all_to_all(slab_output(lax.all_to_all(forward, 'local', split_axis=0,...  50.8 us
    all_to_all x1, waiting for transfers between devices, on_device(): lax.all_to_all(forward, 'local', split_axis=0, concat_axis=0, tiled=True)  50.1 us
    all_to_all x1, blocking collectives, on_device(): lax.all_to_all(merged.astype(jnp.bfloat16), 'node', split_axis=0, concat_...  16.9 us
    all_to_all x1, blocking collectives, on_device(): lax.all_to_all(rows_out, 'node', split_axis=0, concat_axis=0, tiled=True)  14 us
    dot_general x1, matrix products, slab_output(): jnp.dot(hidden, down_slab, preferred_element_type=jnp.float32)  10.4 us
    reshape x2, local copies, waits for them, and re-layouts, slab_output(): return result.reshape(packed.shape[:-1] + (down_slab.shape[1],))  9.99 us
    all_to_all x1, starting transfers between devices, on_device(): lax.all_to_all(slab_output(lax.all_to_all(forward, 'local', split_axis=0,...  6.84 us
    dot_general x1, matrix products, slab_output(): gate_act = jnp.dot(flat_rows, gate_slab, preferred_element_type=jnp.float32)  5.53 us
  transfers between devices with their start and end apart: 4, of which 3 were waited for; matrix products, arithmetic and copies ran while one was open for 17% of the time, Pallas kernels for 0%

commit v1 on v0

v1 whole, which is shorter than its diff:
```python
import functools

import jax
import jax.numpy as jnp
from jax import lax
from jax.experimental import pallas as pl
from jax.experimental.pallas import tpu as pltpu
from jax.sharding import PartitionSpec as P

GROUP = 4
CAP = 5
SUB = 16
SPLIT = 3
COL = 256
BF = jnp.bfloat16
F32 = jnp.float32
MESH = pl.DeviceIdType.MESH


def dot(a, b):
    return jnp.dot(a, b, preferred_element_type=F32)


def dot_t(a, b):
    return lax.dot_general(a, b, (((1,), (1,)), ((), ())), preferred_element_type=F32)


def iota(shape, dim):
    return lax.broadcasted_iota(jnp.int32, shape, dim)


def div_cap(x):
    return (x * 205) >> 10


def kernel(
    dims,
    tok_hbm, ids_ref, gates_ref, limits_ref, wg_hbm, wu_hbm, wd_hbm,
    out_ref,
    tok, wg, wu, wd, pack, x, xu, own, sib, sib_in, par_in, home,
    in_sem, recv_x, send_d, send_s, send_r, send_p, recv_p, send_q, recv_q, send_h, recv_h,
):
    nodes, locs = dims
    groups = locs // GROUP
    units = locs // 2
    hosted = nodes * groups
    rows = tok.shape[0]
    width = tok.shape[1]
    piece = x.shape[-1]
    tail0 = SPLIT * piece
    cols = piece // COL
    packed = hosted * SUB
    srcs = 2 * nodes
    chunk = srcs * SUB
    xrows = xu.shape[0]

    node = lax.axis_index("node")
    loc = lax.axis_index("local")
    core = lax.rem(loc, 2)
    unit = loc // 2
    place = lax.rem(unit, 2)
    group = unit // 2
    sibling = (node, unit * 2 + (1 - core))
    partner = (node, group * GROUP + 2 * (1 - place) + core)

    loads = [
        pltpu.make_async_copy(tok_hbm, tok, in_sem.at[0]),
        pltpu.make_async_copy(wg_hbm, wg, in_sem.at[1]),
        pltpu.make_async_copy(wu_hbm, wu, in_sem.at[2]),
        pltpu.make_async_copy(wd_hbm, wd, in_sem.at[3]),
    ]
    for load in loads:
        load.start()

    barrier = pltpu.get_barrier_semaphore()

    def greet(i, _):
        n, u = i // units, lax.rem(i, units)

        @pl.when(jnp.logical_or(n != node, u != unit))
        def _():
            pl.semaphore_signal(barrier, inc=1, device_id=(n, u * 2 + core), device_id_type=MESH)

        return 0

    lax.fori_loop(0, nodes * units, greet, 0)
    pl.semaphore_signal(barrier, inc=1, device_id=sibling, device_id_type=MESH)

    ep = 128
    expert = iota((ep, rows), 0)
    named = jnp.zeros((ep, rows), F32)
    gate = jnp.zeros((ep, rows), F32)
    for k in range(ids_ref.shape[0]):
        hit = ids_ref[k : k + 1, :] == expert
        named = named + jnp.where(hit, 1.0, 0.0)
        gate = gate + jnp.where(hit, gates_ref[k : k + 1, :].astype(F32), 0.0)
    earlier = jnp.where(iota((rows, rows), 0) < iota((rows, rows), 1), 1.0, 0.0).astype(BF)
    before = dot(named.astype(BF), earlier)
    lim = jnp.where(iota((ep, ep), 0) == iota((ep, ep), 1), limits_ref[:, :ep].astype(F32), 0.0)
    lim = jnp.sum(lim, axis=1, keepdims=True)
    kept = jnp.logical_and(named > 0.5, before < lim)
    slot = jnp.where(kept, before, -1.0)
    coef = jnp.where(kept, gate, 0.0)
    spread = jnp.where(iota((packed, ep), 0) // SUB == iota((packed, ep), 1), 1.0, 0.0).astype(BF)
    slot_m = dot(spread, slot.astype(BF))
    coef_m = dot(spread, coef.astype(BF))

    def member(line, slots, q):
        row = lax.rem(line, SUB)
        rank = (row * 11) >> 5
        ok = jnp.logical_and(row < SUB - 1, row - SPLIT * rank == q)
        return jnp.logical_and(ok, slots == rank.astype(F32))

    def member_tail(line, slots, r):
        return jnp.logical_and(lax.rem(line, SUB) == SUB - 1, slots == float(r))

    line = iota((packed, rows), 0)
    heads = [jnp.where(member(line, slot_m, q), 1.0, 0.0).astype(BF) for q in range(SPLIT)]
    tails = [jnp.where(member_tail(line, slot_m, r), 1.0, 0.0).astype(BF) for r in range(CAP)]

    loads[0].wait()
    for j in range(cols):
        acc = dot(heads[0], tok[:, j * COL : (j + 1) * COL])
        for q in range(1, SPLIT):
            acc = acc + dot(heads[q], tok[:, q * piece + j * COL : q * piece + (j + 1) * COL])
        if j < CAP:
            acc = acc + dot(tails[j], tok[:, tail0:])
        pack[:, :, j * COL : (j + 1) * COL] = acc.astype(BF).reshape(hosted, SUB, COL)

    pl.semaphore_wait(barrier, nodes * units)

    def near_place(src_group, src_place, g):
        return jnp.where(src_group < g, 0, jnp.where(src_group > g, 1, src_place))

    def target(i):
        g = lax.rem(group + 1 + i // nodes, groups)
        n = lax.rem(node + 1 + lax.rem(i, nodes), nodes)
        to_unit = 2 * g + near_place(group, place, g)
        e = n * groups + g
        return e, n, to_unit, jnp.logical_and(n == node, to_unit == unit)

    def dispatch(e, n, to_unit):
        return pltpu.make_async_remote_copy(
            src_ref=pack.at[e], dst_ref=x.at[unit, core, node], send_sem=send_d.at[e],
            recv_sem=recv_x.at[unit, core, node], device_id=(n, 2 * to_unit + core), device_id_type=MESH,
        )

    def send_out(i, _):
        e, n, to_unit, mine = target(i)

        @pl.when(mine)
        def _():
            pltpu.make_async_copy(pack.at[e], x.at[unit, core, node], recv_x.at[unit, core, node]).start()

        @pl.when(jnp.logical_not(mine))
        def _():
            dispatch(e, n, to_unit).start()

        return 0

    lax.fori_loop(0, hosted, send_out, 0)

    at_row, at_line = iota((xrows, chunk), 0), iota((xrows, chunk), 1)
    first = SUB * div_cap(at_row)
    rank = at_row - CAP * div_cap(at_row)
    open_all = jnp.concatenate(
        [jnp.where(at_line == first + SPLIT * rank + q, 1.0, 0.0).astype(BF) for q in range(SPLIT)], axis=0
    )
    open_tail = [
        jnp.where(jnp.logical_and(at_line == first + SUB - 1, rank == r), 1.0, 0.0).astype(BF) for r in range(CAP)
    ]
    at_line, at_row = iota((chunk, xrows), 0), iota((chunk, xrows), 1)
    src = lax.rem(at_line // SUB + core * nodes, srcs)
    sub_row = lax.rem(at_line, SUB)
    rank_of = at_row - CAP * div_cap(at_row)
    same = src == div_cap(at_row)
    close = [
        jnp.where(jnp.logical_and(same, sub_row == SPLIT * rank_of + q), 1.0, 0.0).astype(BF) for q in range(SPLIT)
    ]
    close_tail = [
        jnp.where(jnp.logical_and(same, jnp.logical_and(sub_row == SUB - 1, rank_of == r)), 1.0, 0.0).astype(BF)
        for r in range(CAP)
    ]

    def unit_at(j):
        return lax.rem(2 * group + j, units)

    def is_near(u):
        return near_place(u // 2, lax.rem(u, 2), group) == place

    def to_sibling(u, n):
        return pltpu.make_async_remote_copy(
            src_ref=x.at[u, core, n], dst_ref=x.at[u, core, n], send_sem=send_s.at[u, n],
            recv_sem=recv_x.at[u, core, n], device_id=sibling, device_id_type=MESH,
        )

    def to_partner(u, n):
        return pltpu.make_async_remote_copy(
            src_ref=x.at[u, core, n], dst_ref=x.at[u, core, n], send_sem=send_r.at[u, n],
            recv_sem=recv_x.at[u, core, n], device_id=partner, device_id_type=MESH,
        )

    def give_half(j, u):
        return pltpu.make_async_remote_copy(
            src_ref=sib.at[lax.rem(j, 2)], dst_ref=sib_in.at[u], send_sem=send_p.at[lax.rem(j, 2)],
            recv_sem=recv_p.at[u], device_id=sibling, device_id_type=MESH,
        )

    def give_sum(u):
        return pltpu.make_async_remote_copy(
            src_ref=own.at[u], dst_ref=par_in.at[u], send_sem=send_q.at[u],
            recv_sem=recv_q.at[u], device_id=partner, device_id_type=MESH,
        )

    expert_here = node * groups + group

    def give_home(u, n):
        return pltpu.make_async_remote_copy(
            src_ref=own.at[u, n], dst_ref=home.at[expert_here], send_sem=send_h.at[u, n],
            recv_sem=recv_h.at[expert_here], device_id=(n, 2 * u + core), device_id_type=MESH,
        )

    def landed(ref, sem):
        pltpu.make_async_copy(ref, ref, sem).wait()

    def compute(j, u):
        tail = jnp.zeros((xrows, COL), F32)
        for c in range(cols):
            xc = x[u, :, :, :, c * COL : (c + 1) * COL].reshape(chunk, COL)
            opened = dot(open_all, xc).astype(BF)
            for q in range(SPLIT):
                xu[:, q * piece + c * COL : q * piece + (c + 1) * COL] = opened[q * xrows : (q + 1) * xrows]
            if c < CAP:
                tail = tail + dot(open_tail[c], xc)
        xu[:, tail0:] = tail.astype(BF)

        @pl.when(j == 0)
        def _():
            for load in loads[1:]:
                load.wait()

        act = dot_t(xu[...], wg[...])
        up = dot_t(xu[...], wu[...])
        hidden = (act / (1.0 + jnp.exp(-act)) * up).astype(BF)
        spreads = [dot(m, hidden).astype(BF) for m in close]
        last = dot(hidden, wd[:, tail0:]).astype(BF)
        b = lax.rem(j, 2)
        for c in range(cols):
            acc = dot(spreads[0], wd[:, c * COL : (c + 1) * COL])
            for q in range(1, SPLIT):
                acc = acc + dot(spreads[q], wd[:, q * piece + c * COL : q * piece + (c + 1) * COL])
            if c < CAP:
                acc = acc + dot(close_tail[c], last)
            parts = acc.astype(BF).reshape(2, nodes, SUB, COL)
            own[u, :, :, c * COL : (c + 1) * COL] = parts[0]
            sib[b, :, :, c * COL : (c + 1) * COL] = parts[1]

    def step(j, _):
        u = unit_at(j)

        @pl.when(j < units)
        def _():
            near = is_near(u)

            def relay(n, _):
                landed(x.at[u, core, n], recv_x.at[u, core, n])

                @pl.when(near)
                def _():
                    to_partner(u, n).start()

                to_sibling(u, n).start()
                return 0

            lax.fori_loop(0, nodes, relay, 0)

            def arrive(n, _):
                landed(x.at[u, 1 - core, n], recv_x.at[u, 1 - core, n])
                return 0

            lax.fori_loop(0, nodes, arrive, 0)

            @pl.when(j >= 2)
            def _():
                give_half(j, u).wait_send()

            compute(j, u)
            give_half(j, u).start()

        @pl.when(jnp.logical_and(j >= 1, j < units + 1))
        def _():
            v = unit_at(j - 1)
            landed(sib_in.at[v], recv_p.at[v])

            @pl.when(jnp.logical_not(is_near(v)))
            def _():
                for n in range(nodes):
                    own[v, n] = (own[v, n].astype(F32) + sib_in[v, n].astype(F32)).astype(BF)
                give_sum(v).start()

        @pl.when(j >= 2)
        def _():
            v = unit_at(j - 2)

            @pl.when(is_near(v))
            def _():
                landed(par_in.at[v], recv_q.at[v])
                for n in range(nodes):
                    total = own[v, n].astype(F32) + sib_in[v, n].astype(F32) + par_in[v, n].astype(F32)
                    own[v, n] = total.astype(BF)

                def back(n, _):
                    mine = jnp.logical_and(n == node, v == unit)

                    @pl.when(mine)
                    def _():
                        pltpu.make_async_copy(own.at[v, n], home.at[expert_here], recv_h.at[expert_here]).start()

                    @pl.when(jnp.logical_not(mine))
                    def _():
                        give_home(v, n).start()

                    return 0

                lax.fori_loop(0, nodes, back, 0)

        return 0

    lax.fori_loop(0, units + 2, step, 0)

    line = iota((rows, packed), 1)
    slot_t = jnp.transpose(slot_m)
    coef_t = jnp.transpose(coef_m)
    heads = [jnp.where(member(line, slot_t, q), coef_t, 0.0).astype(BF) for q in range(SPLIT)]
    tails = [jnp.where(member_tail(line, slot_t, r), coef_t, 0.0).astype(BF) for r in range(CAP)]

    def returned(e, _):
        landed(home.at[e], recv_h.at[e])
        return 0

    lax.fori_loop(0, hosted, returned, 0)
    tail = jnp.zeros((rows, COL), F32)
    for c in range(cols):
        got = home[:, :, c * COL : (c + 1) * COL].reshape(packed, COL)
        for q in range(SPLIT):
            out_ref[:, q * piece + c * COL : q * piece + (c + 1) * COL] = dot(heads[q], got).astype(BF)
        if c < CAP:
            tail = tail + dot(tails[c], got)
    out_ref[:, tail0:] = tail.astype(BF)

    def sent(i, _):
        e, n, to_unit, mine = target(i)

        @pl.when(jnp.logical_not(mine))
        def _():
            dispatch(e, n, to_unit).wait_send()

        return 0

    lax.fori_loop(0, hosted, sent, 0)

    def drained(u, _):
        near = is_near(u)

        def each(n, _):
            to_sibling(u, n).wait_send()

            @pl.when(near)
            def _():
                to_partner(u, n).wait_send()

            @pl.when(jnp.logical_and(near, jnp.logical_or(n != node, u != unit)))
            def _():
                give_home(u, n).wait_send()

            return 0

        lax.fori_loop(0, nodes, each, 0)

        @pl.when(jnp.logical_not(near))
        def _():
            give_sum(u).wait_send()

        return 0

    lax.fori_loop(0, units, drained, 0)
    for j in range(max(units - 2, 0), units):
        give_half(j, 0).wait_send()


def on_device(tokens, route_ids, route_gates, limits, w_gate, w_up, w_down):
    nodes = lax.axis_size("node")
    locs = lax.axis_size("local")
    units = locs // 2
    hosted = nodes * (locs // GROUP)
    rows, width = tokens.shape
    slab = w_down.shape[1]
    piece = (width // COL // SPLIT) * COL
    assert width - SPLIT * piece == COL and SPLIT * CAP == SUB - 1
    assert CAP * COL <= piece and hosted <= 128
    xrows = -(-2 * nodes * CAP // SUB) * SUB
    block = (SUB, piece)
    dma = pltpu.SemaphoreType.DMA
    vmem = pl.BlockSpec(memory_space=pltpu.VMEM)
    hbm = pl.BlockSpec(memory_space=pl.ANY)
    return pl.pallas_call(
        functools.partial(kernel, (nodes, locs)),
        out_shape=jax.ShapeDtypeStruct((rows, width), BF),
        in_specs=[hbm, vmem, vmem, vmem, hbm, hbm, hbm],
        out_specs=vmem,
        scratch_shapes=[
            pltpu.VMEM((rows, width), BF),
            pltpu.VMEM((slab, width), BF),
            pltpu.VMEM((slab, width), BF),
            pltpu.VMEM((slab, width), BF),
            pltpu.VMEM((hosted,) + block, BF),
            pltpu.VMEM((units, 2, nodes) + block, BF),
            pltpu.VMEM((xrows, width), BF),
            pltpu.VMEM((units, nodes) + block, BF),
            pltpu.VMEM((2, nodes) + block, BF),
            pltpu.VMEM((units, nodes) + block, BF),
            pltpu.VMEM((units, nodes) + block, BF),
            pltpu.VMEM((hosted,) + block, BF),
            dma((4,)),
            dma((units, 2, nodes)),
            dma((hosted,)),
            dma((units, nodes)),
            dma((units, nodes)),
            dma((2,)),
            dma((units,)),
            dma((units,)),
            dma((units,)),
            dma((units, nodes)),
            dma((hosted,)),
        ],
        compiler_params=pltpu.CompilerParams(
            collective_id=0, has_side_effects=True, vmem_limit_bytes=60 * 1024 * 1024
        ),
        cost_estimate=pl.CostEstimate(
            flops=6 * locs * nodes * CAP * width * slab, bytes_accessed=6 * width * slab, transcendentals=0
        ),
    )(
        tokens,
        route_ids.T,
        route_gates.T,
        limits.reshape(1, -1),
        jnp.swapaxes(w_gate, 1, 2)[0],
        jnp.swapaxes(w_up, 1, 2)[0],
        w_down[0],
    )


def solution(mesh):
    return jax.shard_map(
        on_device,
        mesh=mesh,
        in_specs=(
            P(("node", "local"), None),
            P(("node", "local"), None),
            P(("node", "local"), None),
            P(),
            P(("node", "local"), None, None),
            P(("node", "local"), None, None),
            P(("node", "local"), None, None),
        ),
        out_specs=P(("node", "local"), None),
        check_vma=False,
    )
```

time: 211 us -> 101 us (0.48)
  the two profiles are of different devices: /device:TPU:24 before, /device:TPU:14 now
where the time goes in v1:
time: 101 us
  Pallas kernels  96.5 us (96%)
  local copies, waits for them, and re-layouts  4.09 us (4%)
    pallas_call x1, Pallas kernels, on_device(): pl.pallas_call(functools.partial(kernel, (nodes, locs)), out_shape=jax.Sh...  96.5 us
    unnamed x1, local copies, waits for them, and re-layouts  2.85 us

profile of v1, /device:TPU:14, one launch (start us, length us, event | category | flops | bytes accessed | tf_op | source)
XLA Modules:
  0.0 100.6 jit_solution(1354571492359451281)
XLA Ops:
  0.0 1.2 %reshape.3.limits_ref = s32[1,384]{1,0:T(1,128)} reshape(s32[384]{0:T(512)} %param.10) | data formatting | bytes 3072 | tf_op jit(solution)/shard_map/reshape | solution.py:446
  1.2 96.5 %shard_map.73 = bf16[128,7168]{1,0:T(8,128)(2,1)} custom-call(bf16[128,7168]{1,0:T(8,128)(2,1)} %tok_hbm.1, s32[8,128]{1,0:T(8,128)} %bitcast.12, bf16[8,128]{1,0:T(8,128)(2,1)} %bitcast.13, s32[1,384]{1,0:T(1,128)} %reshape.3.limits_ref, bf16[448,7168]{1,0:T(8,128)(2,1)} %bitcast.9, bf16[448,7168]{1,0:T(8,128)(2,1)} %bitcast.10, bf16[448,7168]{1,0:T(8,128)(2,1)} %bitcast.11), custom_call_target="tpu_custom_call" | custom-call | flops 3082813440 | bytes 19267584 | tf_op jit(solution)/shard_map/pallas_call | solution.py:406
  97.8 2.8 %copy.9 = bf16[128,7168]{1,0:T(8,128)(2,1)} copy(bf16[128,7168]{1,0:T(8,128)(2,1)} %shard_map.73) | data formatting | bytes 3670016

commit v2 on v1

--- a/solution.py
+++ b/solution.py
@@ -9,6 +9,7 @@
 
 GROUP = 4
 CAP = 5
+PAIR = 2
 SUB = 16
 SPLIT = 3
 COL = 256
@@ -50,7 +51,8 @@
     tail0 = SPLIT * piece
     cols = piece // COL
     packed = hosted * SUB
-    srcs = 2 * nodes
+    srcs = PAIR * 2 * nodes
+    steps = units // PAIR
     chunk = srcs * SUB
     xrows = xu.shape[0]
 
@@ -69,8 +71,7 @@
         pltpu.make_async_copy(wu_hbm, wu, in_sem.at[2]),
         pltpu.make_async_copy(wd_hbm, wd, in_sem.at[3]),
     ]
-    for load in loads:
-        load.start()
+    loads[0].start()
 
     barrier = pltpu.get_barrier_semaphore()
 
@@ -96,8 +97,9 @@
         gate = gate + jnp.where(hit, gates_ref[k : k + 1, :].astype(F32), 0.0)
     earlier = jnp.where(iota((rows, rows), 0) < iota((rows, rows), 1), 1.0, 0.0).astype(BF)
     before = dot(named.astype(BF), earlier)
-    lim = jnp.where(iota((ep, ep), 0) == iota((ep, ep), 1), limits_ref[:, :ep].astype(F32), 0.0)
-    lim = jnp.sum(lim, axis=1, keepdims=True)
+    lim = jnp.zeros((ep, rows), F32)
+    for e in range(hosted):
+        lim = jnp.where(expert == e, limits_ref[e].astype(F32), lim)
     kept = jnp.logical_and(named > 0.5, before < lim)
     slot = jnp.where(kept, before, -1.0)
     coef = jnp.where(kept, gate, 0.0)
@@ -119,6 +121,8 @@
     tails = [jnp.where(member_tail(line, slot_m, r), 1.0, 0.0).astype(BF) for r in range(CAP)]
 
     loads[0].wait()
+    for load in loads[1:]:
+        load.start()
     for j in range(cols):
         acc = dot(heads[0], tok[:, j * COL : (j + 1) * COL])
         for q in range(1, SPLIT):
@@ -133,8 +137,8 @@
         return jnp.where(src_group < g, 0, jnp.where(src_group > g, 1, src_place))
 
     def target(i):
-        g = lax.rem(group + 1 + i // nodes, groups)
-        n = lax.rem(node + 1 + lax.rem(i, nodes), nodes)
+        g = lax.rem(group + lax.rem(i, groups), groups)
+        n = lax.rem(node + i // groups, nodes)
         to_unit = 2 * g + near_place(group, place, g)
         e = n * groups + g
         return e, n, to_unit, jnp.logical_and(n == node, to_unit == unit)
@@ -170,7 +174,9 @@
         jnp.where(jnp.logical_and(at_line == first + SUB - 1, rank == r), 1.0, 0.0).astype(BF) for r in range(CAP)
     ]
     at_line, at_row = iota((chunk, xrows), 0), iota((chunk, xrows), 1)
-    src = lax.rem(at_line // SUB + core * nodes, srcs)
+    blk = at_line // SUB
+    half = blk // (PAIR * nodes)
+    src = lax.rem(blk // nodes, PAIR) * (2 * nodes) + lax.rem(core + half, 2) * nodes + lax.rem(blk, nodes)
     sub_row = lax.rem(at_line, SUB)
     rank_of = at_row - CAP * div_cap(at_row)
     same = src == div_cap(at_row)
@@ -183,7 +189,7 @@
     ]
 
     def unit_at(j):
-        return lax.rem(2 * group + j, units)
+        return lax.rem(2 * group + PAIR * j, units)
 
     def is_near(u):
         return near_place(u // 2, lax.rem(u, 2), group) == place
@@ -200,9 +206,10 @@
             recv_sem=recv_x.at[u, core, n], device_id=partner, device_id_type=MESH,
         )
 
-    def give_half(j, u):
-        return pltpu.make_async_remote_copy(
-            src_ref=sib.at[lax.rem(j, 2)], dst_ref=sib_in.at[u], send_sem=send_p.at[lax.rem(j, 2)],
+    def give_half(j, k):
+        b, u = lax.rem(j, 2), unit_at(j) + k
+        return pltpu.make_async_remote_copy(
+            src_ref=sib.at[b, k], dst_ref=sib_in.at[u], send_sem=send_p.at[b, k],
             recv_sem=recv_p.at[u], device_id=sibling, device_id_type=MESH,
         )
 
@@ -223,10 +230,65 @@
     def landed(ref, sem):
         pltpu.make_async_copy(ref, ref, sem).wait()
 
-    def compute(j, u):
+    def relay(j, k):
+        u, n = unit_at(j) + k // nodes, lax.rem(node + nodes - lax.rem(k, nodes), nodes)
+        landed(x.at[u, core, n], recv_x.at[u, core, n])
+
+        @pl.when(is_near(u))
+        def _():
+            to_partner(u, n).start()
+
+        to_sibling(u, n).start()
+
+    def relay_next(j, ks):
+        @pl.when(j + 1 < steps)
+        def _():
+            for k in ks:
+                relay(j + 1, k)
+
+    def add_core(j):
+        for k in range(PAIR):
+            v = unit_at(j) + k
+            landed(sib_in.at[v], recv_p.at[v])
+
+            @pl.when(jnp.logical_not(is_near(v)))
+            def _():
+                for n in range(nodes):
+                    own[v, n] = (own[v, n].astype(F32) + sib_in[v, n].astype(F32)).astype(BF)
+                give_sum(v).start()
+
+    def add_chip(j):
+        for k in range(PAIR):
+            v = unit_at(j) + k
+
+            @pl.when(is_near(v))
+            def _():
+                landed(par_in.at[v], recv_q.at[v])
+                for n in range(nodes):
+                    total = own[v, n].astype(F32) + sib_in[v, n].astype(F32) + par_in[v, n].astype(F32)
+                    own[v, n] = total.astype(BF)
+                    mine = jnp.logical_and(n == node, v == unit)
+
+                    @pl.when(mine)
+                    def _():
+                        pltpu.make_async_copy(own.at[v, n], home.at[expert_here], recv_h.at[expert_here]).start()
+
+                    @pl.when(jnp.logical_not(mine))
+                    def _():
+                        give_home(v, n).start()
+
+    def step(j, _):
+        u = unit_at(j)
+
+        def arrive(i, _):
+            v, n = u + i // nodes, lax.rem(i, nodes)
+            landed(x.at[v, 1 - core, n], recv_x.at[v, 1 - core, n])
+            return 0
+
+        lax.fori_loop(0, PAIR * nodes, arrive, 0)
         tail = jnp.zeros((xrows, COL), F32)
         for c in range(cols):
-            xc = x[u, :, :, :, c * COL : (c + 1) * COL].reshape(chunk, COL)
+            xc = x[pl.ds(u, PAIR), :, :, :, c * COL : (c + 1) * COL].reshape(chunk, COL)
             opened = dot(open_all, xc).astype(BF)
             for q in range(SPLIT):
                 xu[:, q * piece + c * COL : q * piece + (c + 1) * COL] = opened[q * xrows : (q + 1) * xrows]
@@ -234,99 +296,60 @@
                 tail = tail + dot(open_tail[c], xc)
         xu[:, tail0:] = tail.astype(BF)
 
+        relays = range(PAIR * nodes)
+        relay_next(j, relays[:2])
+
         @pl.when(j == 0)
         def _():
             for load in loads[1:]:
                 load.wait()
 
-        act = dot_t(xu[...], wg[...])
-        up = dot_t(xu[...], wu[...])
+        act = dot_t(wg[...], xu[...])
+        relay_next(j, relays[2:4])
+        up = dot_t(wu[...], xu[...])
         hidden = (act / (1.0 + jnp.exp(-act)) * up).astype(BF)
-        spreads = [dot(m, hidden).astype(BF) for m in close]
-        last = dot(hidden, wd[:, tail0:]).astype(BF)
+        relay_next(j, relays[4:6])
+
+        @pl.when(j >= 1)
+        def _():
+            add_core(j - 1)
+
+        @pl.when(j >= 2)
+        def _():
+            for k in range(PAIR):
+                give_half(j - 2, k).wait_send()
+
+        spreads = [dot_t(m, hidden).astype(BF) for m in close]
+        spread_tails = [dot_t(m, hidden).astype(BF) for m in close_tail]
         b = lax.rem(j, 2)
         for c in range(cols):
             acc = dot(spreads[0], wd[:, c * COL : (c + 1) * COL])
             for q in range(1, SPLIT):
                 acc = acc + dot(spreads[q], wd[:, q * piece + c * COL : q * piece + (c + 1) * COL])
             if c < CAP:
-                acc = acc + dot(close_tail[c], last)
-            parts = acc.astype(BF).reshape(2, nodes, SUB, COL)
-            own[u, :, :, c * COL : (c + 1) * COL] = parts[0]
-            sib[b, :, :, c * COL : (c + 1) * COL] = parts[1]
-
-    def step(j, _):
-        u = unit_at(j)
-
-        @pl.when(j < units)
-        def _():
-            near = is_near(u)
-
-            def relay(n, _):
-                landed(x.at[u, core, n], recv_x.at[u, core, n])
-
-                @pl.when(near)
-                def _():
-                    to_partner(u, n).start()
-
-                to_sibling(u, n).start()
-                return 0
-
-            lax.fori_loop(0, nodes, relay, 0)
-
-            def arrive(n, _):
-                landed(x.at[u, 1 - core, n], recv_x.at[u, 1 - core, n])
-                return 0
-
-            lax.fori_loop(0, nodes, arrive, 0)
-
-            @pl.when(j >= 2)
-            def _():
-                give_half(j, u).wait_send()
-
-            compute(j, u)
-            give_half(j, u).start()
-
-        @pl.when(jnp.logical_and(j >= 1, j < units + 1))
-        def _():
-            v = unit_at(j - 1)
-            landed(sib_in.at[v], recv_p.at[v])
-
-            @pl.when(jnp.logical_not(is_near(v)))
-            def _():
-                for n in range(nodes):
-                    own[v, n] = (own[v, n].astype(F32) + sib_in[v, n].astype(F32)).astype(BF)
-                give_sum(v).start()
-
-        @pl.when(j >= 2)
-        def _():
-            v = unit_at(j - 2)
-
-            @pl.when(is_near(v))
-            def _():
-                landed(par_in.at[v], recv_q.at[v])
-                for n in range(nodes):
-                    total = own[v, n].astype(F32) + sib_in[v, n].astype(F32) + par_in[v, n].astype(F32)
-                    own[v, n] = total.astype(BF)
-
-                def back(n, _):
-                    mine = jnp.logical_and(n == node, v == unit)
-
-                    @pl.when(mine)
-                    def _():
-                        pltpu.make_async_copy(own.at[v, n], home.at[expert_here], recv_h.at[expert_here]).start()
-
-                    @pl.when(jnp.logical_not(mine))
-                    def _():
-                        give_home(v, n).start()
-
-                    return 0
-
-                lax.fori_loop(0, nodes, back, 0)
-
-        return 0
-
-    lax.fori_loop(0, units + 2, step, 0)
+                acc = acc + dot(spread_tails[c], wd[:, tail0:])
+            parts = acc.astype(BF).reshape(2, PAIR, nodes, SUB, COL)
+            own[pl.ds(u, PAIR), :, :, c * COL : (c + 1) * COL] = parts[0]
+            sib[b, :, :, :, c * COL : (c + 1) * COL] = parts[1]
+            if c == cols // 2:
+                relay_next(j, relays[6:])
+        for k in range(PAIR):
+            give_half(j, k).start()
+
+        @pl.when(j >= 1)
+        def _():
+            add_chip(j - 1)
+
+        return 0
+
+    def relay_first(k, _):
+        relay(0, k)
+        return 0
+
+    lax.fori_loop(0, PAIR * nodes, relay_first, 0)
+    lax.fori_loop(0, steps, step, 0)
+    add_core(steps - 1)
+    add_chip(steps - 1)
 
     line = iota((rows, packed), 1)
     slot_t = jnp.transpose(slot_m)
@@ -384,8 +407,9 @@
         return 0
 
     lax.fori_loop(0, units, drained, 0)
-    for j in range(max(units - 2, 0), units):
-        give_half(j, 0).wait_send()
+    for j in range(max(steps - 2, 0), steps):
+        for k in range(PAIR):
+            give_half(j, k).wait_send()
 
 
 def on_device(tokens, route_ids, route_gates, limits, w_gate, w_up, w_down):
@@ -398,7 +422,8 @@
     piece = (width // COL // SPLIT) * COL
     assert width - SPLIT * piece == COL and SPLIT * CAP == SUB - 1
     assert CAP * COL <= piece and hosted <= 128
-    xrows = -(-2 * nodes * CAP // SUB) * SUB
+    xrows = -(-PAIR * 2 * nodes * CAP // 128) * 128
+    assert units % PAIR == 0 and GROUP == 2 * PAIR
     block = (SUB, piece)
     dma = pltpu.SemaphoreType.DMA
     vmem = pl.BlockSpec(memory_space=pltpu.VMEM)
@@ -406,7 +431,7 @@
     return pl.pallas_call(
         functools.partial(kernel, (nodes, locs)),
         out_shape=jax.ShapeDtypeStruct((rows, width), BF),
-        in_specs=[hbm, vmem, vmem, vmem, hbm, hbm, hbm],
+        in_specs=[hbm, vmem, vmem, pl.BlockSpec(memory_space=pltpu.SMEM), hbm, hbm, hbm],
         out_specs=vmem,
         scratch_shapes=[
             pltpu.VMEM((rows, width), BF),
@@ -417,7 +442,7 @@
             pltpu.VMEM((units, 2, nodes) + block, BF),
             pltpu.VMEM((xrows, width), BF),
             pltpu.VMEM((units, nodes) + block, BF),
-            pltpu.VMEM((2, nodes) + block, BF),
+            pltpu.VMEM((2, PAIR, nodes) + block, BF),
             pltpu.VMEM((units, nodes) + block, BF),
             pltpu.VMEM((units, nodes) + block, BF),
             pltpu.VMEM((hosted,) + block, BF),
@@ -426,7 +451,7 @@
             dma((hosted,)),
             dma((units, nodes)),
             dma((units, nodes)),
-            dma((2,)),
+            dma((2, PAIR)),
             dma((units,)),
             dma((units,)),
             dma((units,)),
@@ -443,7 +468,7 @@
         tokens,
         route_ids.T,
         route_gates.T,
-        limits.reshape(1, -1),
+        limits,
         jnp.swapaxes(w_gate, 1, 2)[0],
         jnp.swapaxes(w_up, 1, 2)[0],
         w_down[0],

time: 101 us -> 84.5 us (0.84)
  the two profiles are of different devices: /device:TPU:14 before, /device:TPU:30 now
where the time goes in v2:
time: 84.5 us; the launch traced here: 84.3 us
  Pallas kernels  81.4 us (96%)
  local copies, waits for them, and re-layouts  2.85 us (3%)
    pallas_call x1, Pallas kernels, on_device(): pl.pallas_call(functools.partial(kernel, (nodes, locs)), out_shape=jax.Sh...  81.4 us
    unnamed x1, local copies, waits for them, and re-layouts  2.85 us

profile of v2, /device:TPU:30, one launch (start us, length us, event | category | flops | bytes accessed | tf_op | source)
XLA Modules:
  0.0 84.3 jit_solution(10908316425075716569)
XLA Ops:
  0.0 81.4 %shard_map.73 = bf16[128,7168]{1,0:T(8,128)(2,1)} custom-call(bf16[128,7168]{1,0:T(8,128)(2,1)} %tok_hbm.1, s32[8,128]{1,0:T(8,128)} %bitcast.12, bf16[8,128]{1,0:T(8,128)(2,1)} %bitcast.13, s32[384]{0:T(512)} %limits_ref.1, bf16[448,7168]{1,0:T(8,128)(2,1)} %bitcast.9, bf16[448,7168]{1,0:T(8,128)(2,1)} %bitcast.10, bf16[448,7168]{1,0:T(8,128)(2,1)} %bitcast.11), custom_call_target="tpu_custom_call" | custom-call | flops 3082813440 | bytes 19267584 | tf_op jit(solution)/shard_map/pallas_call | solution.py:431
  81.4 2.8 %copy.9 = bf16[128,7168]{1,0:T(8,128)(2,1)} copy(bf16[128,7168]{1,0:T(8,128)(2,1)} %shard_map.73) | data formatting | bytes 3670016

commit v3 on v1

v3 whole, which is shorter than its diff:
```python
import functools

import jax
import jax.numpy as jnp
from jax import lax
from jax.experimental import pallas as pl
from jax.experimental.pallas import tpu as pltpu
from jax.sharding import PartitionSpec as P

GROUP = 4
CAP = 5
PIECES = 3
UNIT_ROWS = 48
SUB = 16
SPLIT = 3
COL = 256
BF = jnp.bfloat16
F32 = jnp.float32
MESH = pl.DeviceIdType.MESH


def dot(a, b):
    return jnp.dot(a, b, preferred_element_type=F32)


def dot_t(a, b):
    return lax.dot_general(a, b, (((1,), (1,)), ((), ())), preferred_element_type=F32)


def iota(shape, dim):
    return lax.broadcasted_iota(jnp.int32, shape, dim)


def div_cap(x):
    return (x * 205) >> 10


def kernel(
    dims,
    tok_hbm, ids_ref, gates_ref, limits_ref, wg_hbm, wu_hbm, wd_hbm,
    out_hbm,
    tok, wg, wu, wd, pack, x, xu, xt, act, up, own, sib, sib_in, par_in, home,
    in_sem, recv_x, recv_g, send_d, send_s, send_r, send_p, recv_p, send_q, recv_q, send_h, recv_h,
):
    nodes, locs = dims
    groups = locs // GROUP
    units = locs // 2
    hosted = nodes * groups
    rows = tok.shape[0]
    pieces, part = x.shape[0], x.shape[-1]
    piece = pieces * part
    tail0 = SPLIT * piece
    cols = part // COL
    packed = hosted * SUB
    chunk = 2 * nodes * SUB
    xrows = xu.shape[0]

    node = lax.axis_index("node")
    loc = lax.axis_index("local")
    core = lax.rem(loc, 2)
    unit = loc // 2
    place = lax.rem(unit, 2)
    group = unit // 2
    sibling = (node, unit * 2 + (1 - core))
    partner = (node, group * GROUP + 2 * (1 - place) + core)

    loads = [
        pltpu.make_async_copy(tok_hbm, tok, in_sem.at[0]),
        pltpu.make_async_copy(wg_hbm, wg, in_sem.at[1]),
        pltpu.make_async_copy(wu_hbm, wu, in_sem.at[2]),
        pltpu.make_async_copy(wd_hbm, wd, in_sem.at[3]),
    ]
    loads[0].start()

    barrier = pltpu.get_barrier_semaphore()

    def greet(i, _):
        n, u = i // units, lax.rem(i, units)

        @pl.when(jnp.logical_or(n != node, u != unit))
        def _():
            pl.semaphore_signal(barrier, inc=1, device_id=(n, u * 2 + core), device_id_type=MESH)

        return 0

    lax.fori_loop(0, nodes * units, greet, 0)
    pl.semaphore_signal(barrier, inc=1, device_id=sibling, device_id_type=MESH)

    ep = 128
    expert = iota((ep, rows), 0)
    named = jnp.zeros((ep, rows), F32)
    gate = jnp.zeros((ep, rows), F32)
    for k in range(ids_ref.shape[0]):
        hit = ids_ref[k : k + 1, :] == expert
        named = named + jnp.where(hit, 1.0, 0.0)
        gate = gate + jnp.where(hit, gates_ref[k : k + 1, :].astype(F32), 0.0)
    earlier = jnp.where(iota((rows, rows), 0) < iota((rows, rows), 1), 1.0, 0.0).astype(BF)
    before = dot(named.astype(BF), earlier)
    lim = jnp.zeros((ep, rows), F32)
    for e in range(hosted):
        lim = jnp.where(expert == e, limits_ref[e].astype(F32), lim)
    kept = jnp.logical_and(named > 0.5, before < lim)
    slot = jnp.where(kept, before, -1.0)
    coef = jnp.where(kept, gate, 0.0)
    spread = jnp.where(iota((packed, ep), 0) // SUB == iota((packed, ep), 1), 1.0, 0.0).astype(BF)
    slot_m = dot(spread, slot.astype(BF))
    coef_m = dot(spread, coef.astype(BF))

    def member(line, slots, q):
        row = lax.rem(line, SUB)
        rank = (row * 11) >> 5
        ok = jnp.logical_and(row < SUB - 1, row - SPLIT * rank == q)
        return jnp.logical_and(ok, slots == rank.astype(F32))

    def member_tail(line, slots, r):
        return jnp.logical_and(lax.rem(line, SUB) == SUB - 1, slots == float(r))

    line = iota((packed, rows), 0)
    heads = [jnp.where(member(line, slot_m, q), 1.0, 0.0).astype(BF) for q in range(SPLIT)]
    tails = [jnp.where(member_tail(line, slot_m, r), 1.0, 0.0).astype(BF) for r in range(CAP)]

    loads[0].wait()
    for load in loads[1:]:
        load.start()

    def near_place(src_group, src_place, g):
        return jnp.where(src_group < g, 0, jnp.where(src_group > g, 1, src_place))

    def target(i):
        g = lax.rem(group + lax.rem(i, groups), groups)
        n = lax.rem(node + i // groups, nodes)
        to_unit = 2 * g + near_place(group, place, g)
        e = n * groups + g
        return e, n, to_unit, jnp.logical_and(n == node, to_unit == unit)

    def dispatch(p, e, n, to_unit):
        return pltpu.make_async_remote_copy(
            src_ref=pack.at[p, e], dst_ref=x.at[p, unit, core, node], send_sem=send_d.at[p, e],
            recv_sem=recv_x.at[p, unit, node], device_id=(n, 2 * to_unit + core), device_id_type=MESH,
        )

    for p in range(pieces):
        for c in range(cols):
            j = p * cols + c
            acc = dot(heads[0], tok[:, j * COL : (j + 1) * COL])
            for q in range(1, SPLIT):
                acc = acc + dot(heads[q], tok[:, q * piece + j * COL : q * piece + (j + 1) * COL])
            if j < CAP:
                acc = acc + dot(tails[j], tok[:, tail0:])
            pack[p, :, :, c * COL : (c + 1) * COL] = acc.astype(BF).reshape(hosted, SUB, COL)
        if p == 0:
            pl.semaphore_wait(barrier, nodes * units)

        def send_out(i, _):
            e, n, to_unit, mine = target(i)

            @pl.when(mine)
            def _():
                pltpu.make_async_copy(pack.at[p, e], x.at[p, unit, core, node], recv_x.at[p, unit, node]).start()

            @pl.when(jnp.logical_not(mine))
            def _():
                dispatch(p, e, n, to_unit).start()

            return 0

        lax.fori_loop(0, hosted, send_out, 0)

    def opener(parts):
        i, m = iota((UNIT_ROWS, chunk), 0), iota((UNIT_ROWS, chunk), 1)
        first, rank = SUB * div_cap(i), i - CAP * div_cap(i)
        out = [m == first + SPLIT * rank + q for q in range(SPLIT)]
        out += [jnp.logical_and(m == first + SUB - 1, rank == r) for r in parts]
        return jnp.concatenate([jnp.where(o, 1.0, 0.0) for o in out], axis=0).astype(BF)

    def closer(parts):
        m, i = iota((chunk, UNIT_ROWS), 0), iota((chunk, UNIT_ROWS), 1)
        blk, sub_row, rank = m // SUB, lax.rem(m, SUB), i - CAP * div_cap(i)
        src = lax.rem(core + blk // nodes, 2) * nodes + lax.rem(blk, nodes)
        same = src == div_cap(i)
        out = [jnp.logical_and(same, sub_row == SPLIT * rank + q) for q in range(SPLIT)]
        out += [jnp.logical_and(same, jnp.logical_and(sub_row == SUB - 1, rank == r)) for r in parts]
        return jnp.concatenate([jnp.where(o, 1.0, 0.0) for o in out], axis=1).astype(BF)

    tail_parts = [[j] if j < CAP else [] for j in range(pieces * cols)]

    def is_near(u):
        return near_place(u // 2, lax.rem(u, 2), group) == place

    def to_sibling(p, u):
        return pltpu.make_async_remote_copy(
            src_ref=x.at[p, u, core], dst_ref=x.at[p, u, core], send_sem=send_s.at[p, u],
            recv_sem=recv_g.at[p, u, core], device_id=sibling, device_id_type=MESH,
        )

    def to_partner(p, u):
        return pltpu.make_async_remote_copy(
            src_ref=x.at[p, u, core], dst_ref=x.at[p, u, core], send_sem=send_r.at[p, u],
            recv_sem=recv_g.at[p, u, core], device_id=partner, device_id_type=MESH,
        )

    def give_half(p):
        return pltpu.make_async_remote_copy(
            src_ref=sib.at[p], dst_ref=sib_in.at[p], send_sem=send_p.at[p],
            recv_sem=recv_p.at[p], device_id=sibling, device_id_type=MESH,
        )

    def give_sum(p, u):
        return pltpu.make_async_remote_copy(
            src_ref=own.at[p, u], dst_ref=par_in.at[p, u], send_sem=send_q.at[p, u],
            recv_sem=recv_q.at[p, u], device_id=partner, device_id_type=MESH,
        )

    expert_here = node * groups + group

    def give_home(p, u, n):
        return pltpu.make_async_remote_copy(
            src_ref=own.at[p, u, n], dst_ref=home.at[p, expert_here], send_sem=send_h.at[p, u, n],
            recv_sem=recv_h.at[p, expert_here], device_id=(n, 2 * u + core), device_id_type=MESH,
        )

    def landed(ref, sem):
        pltpu.make_async_copy(ref, ref, sem).wait()

    def relay(p):
        def first(k, _):
            u = lax.rem(2 * group + k, units)

            @pl.when(is_near(u))
            def _():
                for n in range(nodes):
                    landed(x.at[p, u, core, n], recv_x.at[p, u, n])
                to_partner(p, u).start()
                to_sibling(p, u).start()

            return 0

        def second(k, _):
            u = lax.rem(2 * group + k, units)

            @pl.when(jnp.logical_not(is_near(u)))
            def _():
                landed(x.at[p, u, core], recv_g.at[p, u, core])
                to_sibling(p, u).start()

            return 0

        def third(k, _):
            u = lax.rem(2 * group + k, units)
            landed(x.at[p, u, 1 - core], recv_g.at[p, u, 1 - core])
            return 0

        lax.fori_loop(0, units, first, 0)
        lax.fori_loop(0, units, second, 0)
        lax.fori_loop(0, units, third, 0)

    if xrows > units * UNIT_ROWS:
        spare = (xrows - units * UNIT_ROWS, xu.shape[1])
        xu[units * UNIT_ROWS :, :] = jnp.zeros(spare, BF)
        xt[units * UNIT_ROWS :, :] = jnp.zeros((spare[0], COL), BF)
    last_tail = (CAP - 1) // cols
    for p in range(pieces):
        relay(p)
        for c in range(cols):
            j = p * cols + c
            opening = opener(tail_parts[j])

            def unpack(u, _):
                base = pl.multiple_of(u * UNIT_ROWS, SUB)
                xc = x[p, u, :, :, :, c * COL : (c + 1) * COL].reshape(chunk, COL)
                opened = dot(opening, xc).astype(BF)
                for q in range(SPLIT):
                    xu[pl.ds(base, UNIT_ROWS), q * part + c * COL : q * part + (c + 1) * COL] = opened[
                        q * UNIT_ROWS : (q + 1) * UNIT_ROWS
                    ]
                if j < CAP:
                    more = opened[SPLIT * UNIT_ROWS :]
                    if j > 0:
                        more = xt[pl.ds(base, UNIT_ROWS), :] + more
                    xt[pl.ds(base, UNIT_ROWS), :] = more
                return 0

            lax.fori_loop(0, units, unpack, 0, unroll=True if units <= 4 else 1)
        if p == 0:
            for load in loads[1:]:
                load.wait()
        for w, total in ((wg, act), (wu, up)):
            acc = dot_t(w[:, p * part : (p + 1) * part], xu[:, :part])
            for q in range(1, SPLIT):
                at = q * piece + p * part
                acc = acc + dot_t(w[:, at : at + part], xu[:, q * part : (q + 1) * part])
            if p == last_tail:
                acc = acc + dot_t(w[:, tail0:], xt[...])
            total[...] = acc if p == 0 else total[...] + acc

    hidden_t = (act[...] / (1.0 + jnp.exp(-act[...])) * up[...]).astype(BF)
    eye = jnp.where(iota((xrows, xrows), 0) == iota((xrows, xrows), 1), 1.0, 0.0).astype(BF)
    hidden = dot_t(eye, hidden_t).astype(BF)
    last = dot(hidden, wd[:, tail0:]).astype(BF)

    def add_core(p):
        landed(sib_in.at[p], recv_p.at[p])

        def far(u, _):
            @pl.when(jnp.logical_not(is_near(u)))
            def _():
                for n in range(nodes):
                    own[p, u, n] = (own[p, u, n].astype(F32) + sib_in[p, u, n].astype(F32)).astype(BF)
                give_sum(p, u).start()

            return 0

        lax.fori_loop(0, units, far, 0)

    def add_chip(p):
        def near(u, _):
            @pl.when(is_near(u))
            def _():
                landed(par_in.at[p, u], recv_q.at[p, u])
                for n in range(nodes):
                    total = own[p, u, n].astype(F32) + sib_in[p, u, n].astype(F32) + par_in[p, u, n].astype(F32)
                    own[p, u, n] = total.astype(BF)
                    mine = jnp.logical_and(n == node, u == unit)

                    @pl.when(mine)
                    def _():
                        pltpu.make_async_copy(
                            own.at[p, u, n], home.at[p, expert_here], recv_h.at[p, expert_here]
                        ).start()

                    @pl.when(jnp.logical_not(mine))
                    def _():
                        give_home(p, u, n).start()

            return 0

        lax.fori_loop(0, units, near, 0)

    for p in range(pieces):
        for c in range(cols):
            j = p * cols + c
            outs = [
                dot(hidden, wd[:, q * piece + j * COL : q * piece + (j + 1) * COL]).astype(BF) for q in range(SPLIT)
            ]
            if j < CAP:
                outs.append(last)
            closing = closer(tail_parts[j])
            for u in range(units):
                mine = [o[u * UNIT_ROWS : (u + 1) * UNIT_ROWS] for o in outs]
                halves = dot(closing, jnp.concatenate(mine, axis=0)).astype(BF).reshape(2, nodes, SUB, COL)
                own[p, u, :, :, c * COL : (c + 1) * COL] = halves[0]
                sib[p, u, :, :, c * COL : (c + 1) * COL] = halves[1]
        give_half(p).start()
        if p >= 1:
            add_core(p - 1)
        if p >= 2:
            add_chip(p - 2)
    add_core(pieces - 1)
    for p in range(max(pieces - 2, 0), pieces):
        add_chip(p)

    line = iota((rows, packed), 1)
    slot_t = jnp.transpose(slot_m)
    coef_t = jnp.transpose(coef_m)
    heads = [jnp.where(member(line, slot_t, q), coef_t, 0.0).astype(BF) for q in range(SPLIT)]
    tails = [jnp.where(member_tail(line, slot_t, r), coef_t, 0.0).astype(BF) for r in range(CAP)]
    tail = jnp.zeros((rows, COL), F32)
    for p in range(pieces):
        def returned(e, _):
            landed(home.at[p, e], recv_h.at[p, e])
            return 0

        lax.fori_loop(0, hosted, returned, 0)
        for c in range(cols):
            j = p * cols + c
            got = home[p, :, :, c * COL : (c + 1) * COL].reshape(packed, COL)
            for q in range(SPLIT):
                tok[:, q * piece + j * COL : q * piece + (j + 1) * COL] = dot(heads[q], got).astype(BF)
            if j < CAP:
                tail = tail + dot(tails[j], got)
    tok[:, tail0:] = tail.astype(BF)
    store = pltpu.make_async_copy(tok, out_hbm, in_sem.at[0])
    store.start()

    for p in range(pieces):
        def sent(i, _):
            e, n, to_unit, mine = target(i)

            @pl.when(jnp.logical_not(mine))
            def _():
                dispatch(p, e, n, to_unit).wait_send()

            return 0

        lax.fori_loop(0, hosted, sent, 0)

        def drained(u, _):
            near = is_near(u)
            to_sibling(p, u).wait_send()

            @pl.when(near)
            def _():
                to_partner(p, u).wait_send()
                for n in range(nodes):
                    @pl.when(jnp.logical_or(n != node, u != unit))
                    def _():
                        give_home(p, u, n).wait_send()

            @pl.when(jnp.logical_not(near))
            def _():
                give_sum(p, u).wait_send()

            return 0

        lax.fori_loop(0, units, drained, 0)
        give_half(p).wait_send()
    store.wait()


def on_device(tokens, route_ids, route_gates, limits, w_gate, w_up, w_down):
    nodes = lax.axis_size("node")
    locs = lax.axis_size("local")
    units = locs // 2
    hosted = nodes * (locs // GROUP)
    rows, width = tokens.shape
    slab = w_down.shape[1]
    piece = (width // COL // SPLIT) * COL
    part = piece // PIECES
    assert width - SPLIT * piece == COL and SPLIT * CAP == SUB - 1 and part * PIECES == piece and part % COL == 0
    assert CAP * COL <= piece and hosted <= 128 and 2 * nodes * CAP <= UNIT_ROWS
    xrows = -(-units * UNIT_ROWS // 128) * 128
    block = (SUB, part)
    dma = pltpu.SemaphoreType.DMA
    vmem = pl.BlockSpec(memory_space=pltpu.VMEM)
    hbm = pl.BlockSpec(memory_space=pl.ANY)
    return pl.pallas_call(
        functools.partial(kernel, (nodes, locs)),
        out_shape=jax.ShapeDtypeStruct((rows, width), BF),
        in_specs=[hbm, vmem, vmem, pl.BlockSpec(memory_space=pltpu.SMEM), hbm, hbm, hbm],
        out_specs=hbm,
        scratch_shapes=[
            pltpu.VMEM((rows, width), BF),
            pltpu.VMEM((slab, width), BF),
            pltpu.VMEM((slab, width), BF),
            pltpu.VMEM((slab, width), BF),
            pltpu.VMEM((PIECES, hosted) + block, BF),
            pltpu.VMEM((PIECES, units, 2, nodes) + block, BF),
            pltpu.VMEM((xrows, SPLIT * part), BF),
            pltpu.VMEM((xrows, COL), BF),
            pltpu.VMEM((slab, xrows), F32),
            pltpu.VMEM((slab, xrows), F32),
            pltpu.VMEM((PIECES, units, nodes) + block, BF),
            pltpu.VMEM((PIECES, units, nodes) + block, BF),
            pltpu.VMEM((PIECES, units, nodes) + block, BF),
            pltpu.VMEM((PIECES, units, nodes) + block, BF),
            pltpu.VMEM((PIECES, hosted) + block, BF),
            dma((4,)),
            dma((PIECES, units, nodes)),
            dma((PIECES, units, 2)),
            dma((PIECES, hosted)),
            dma((PIECES, units)),
            dma((PIECES, units)),
            dma((PIECES,)),
            dma((PIECES,)),
            dma((PIECES, units)),
            dma((PIECES, units)),
            dma((PIECES, units, nodes)),
            dma((PIECES, hosted)),
        ],
        compiler_params=pltpu.CompilerParams(
            collective_id=0, has_side_effects=True, vmem_limit_bytes=62 * 1024 * 1024
        ),
        cost_estimate=pl.CostEstimate(
            flops=6 * locs * nodes * CAP * width * slab, bytes_accessed=6 * width * slab, transcendentals=0
        ),
    )(
        tokens,
        route_ids.T,
        route_gates.T,
        limits,
        jnp.swapaxes(w_gate, 1, 2)[0],
        jnp.swapaxes(w_up, 1, 2)[0],
        w_down[0],
    )


def solution(mesh):
    return jax.shard_map(
        on_device,
        mesh=mesh,
        in_specs=(
            P(("node", "local"), None),
            P(("node", "local"), None),
            P(("node", "local"), None),
            P(),
            P(("node", "local"), None, None),
            P(("node", "local"), None, None),
            P(("node", "local"), None, None),
        ),
        out_specs=P(("node", "local"), None),
        check_vma=False,
    )
```

time: 101 us -> 75.6 us (0.75)
  the two profiles are of different devices: /device:TPU:14 before, /device:TPU:24 now
where the time goes in v3:
time: 75.6 us; the launch traced here: 75.4 us
  Pallas kernels  72.6 us (96%)
  local copies, waits for them, and re-layouts  2.85 us (4%)
    pallas_call x1, Pallas kernels, on_device(): pl.pallas_call(functools.partial(kernel, (nodes, locs)), out_shape=jax.Sh...  72.6 us
    unnamed x1, local copies, waits for them, and re-layouts  2.85 us

profile of v3, /device:TPU:24, one launch (start us, length us, event | category | flops | bytes accessed | tf_op | source)
XLA Modules:
  0.0 75.4 jit_solution(33379672784748436)
XLA Ops:
  0.0 72.6 %shard_map.73 = bf16[128,7168]{1,0:T(8,128)(2,1)} custom-call(bf16[128,7168]{1,0:T(8,128)(2,1)} %tok_hbm.1, s32[8,128]{1,0:T(8,128)} %bitcast.12, bf16[8,128]{1,0:T(8,128)(2,1)} %bitcast.13, s32[384]{0:T(512)} %limits_ref.1, bf16[448,7168]{1,0:T(8,128)(2,1)} %bitcast.9, bf16[448,7168]{1,0:T(8,128)(2,1)} %bitcast.10, bf16[448,7168]{1,0:T(8,128)(2,1)} %bitcast.11), custom_call_target="tpu_custom_call" | custom-call | flops 3082813440 | bytes 19267584 | tf_op jit(solution)/shard_map/pallas_call | solution.py:436
  72.6 2.8 %copy.9 = bf16[128,7168]{1,0:T(8,128)(2,1)} copy(bf16[128,7168]{1,0:T(8,128)(2,1)} %shard_map.73) | data formatting | bytes 3670016

commit v4 on v3

--- a/solution.py
+++ b/solution.py
@@ -39,7 +39,7 @@
     dims,
     tok_hbm, ids_ref, gates_ref, limits_ref, wg_hbm, wu_hbm, wd_hbm,
     out_hbm,
-    tok, wg, wu, wd, pack, x, xu, xt, act, up, own, sib, sib_in, par_in, home,
+    tok, wgu, wd, pack, x, xu, xt, both, own, sib, sib_in, par_in, home,
     in_sem, recv_x, recv_g, send_d, send_s, send_r, send_p, recv_p, send_q, recv_q, send_h, recv_h,
 ):
     nodes, locs = dims
@@ -54,6 +54,7 @@
     packed = hosted * SUB
     chunk = 2 * nodes * SUB
     xrows = xu.shape[0]
+    slab = wd.shape[0]
 
     node = lax.axis_index("node")
     loc = lax.axis_index("local")
@@ -66,8 +67,8 @@
 
     loads = [
         pltpu.make_async_copy(tok_hbm, tok, in_sem.at[0]),
-        pltpu.make_async_copy(wg_hbm, wg, in_sem.at[1]),
-        pltpu.make_async_copy(wu_hbm, wu, in_sem.at[2]),
+        pltpu.make_async_copy(wg_hbm, wgu.at[pl.ds(0, slab)], in_sem.at[1]),
+        pltpu.make_async_copy(wu_hbm, wgu.at[pl.ds(slab, slab)], in_sem.at[2]),
         pltpu.make_async_copy(wd_hbm, wd, in_sem.at[3]),
     ]
     loads[0].start()
@@ -222,7 +223,7 @@
     def landed(ref, sem):
         pltpu.make_async_copy(ref, ref, sem).wait()
 
-    def relay(p):
+    def relay_near(p):
         def first(k, _):
             u = lax.rem(2 * group + k, units)
 
@@ -235,6 +236,9 @@
 
             return 0
 
+        lax.fori_loop(0, units, first, 0)
+
+    def relay_far(p):
         def second(k, _):
             u = lax.rem(2 * group + k, units)
 
@@ -250,7 +254,6 @@
             landed(x.at[p, u, 1 - core], recv_g.at[p, u, 1 - core])
             return 0
 
-        lax.fori_loop(0, units, first, 0)
         lax.fori_loop(0, units, second, 0)
         lax.fori_loop(0, units, third, 0)
 
@@ -259,8 +262,9 @@
         xu[units * UNIT_ROWS :, :] = jnp.zeros(spare, BF)
         xt[units * UNIT_ROWS :, :] = jnp.zeros((spare[0], COL), BF)
     last_tail = (CAP - 1) // cols
+    relay_near(0)
     for p in range(pieces):
-        relay(p)
+        relay_far(p)
         for c in range(cols):
             j = p * cols + c
             opening = opener(tail_parts[j])
@@ -284,17 +288,22 @@
         if p == 0:
             for load in loads[1:]:
                 load.wait()
-        for w, total in ((wg, act), (wu, up)):
-            acc = dot_t(w[:, p * part : (p + 1) * part], xu[:, :part])
-            for q in range(1, SPLIT):
-                at = q * piece + p * part
-                acc = acc + dot_t(w[:, at : at + part], xu[:, q * part : (q + 1) * part])
-            if p == last_tail:
-                acc = acc + dot_t(w[:, tail0:], xt[...])
-            total[...] = acc if p == 0 else total[...] + acc
-
-    hidden_t = (act[...] / (1.0 + jnp.exp(-act[...])) * up[...]).astype(BF)
-    eye = jnp.where(iota((xrows, xrows), 0) == iota((xrows, xrows), 1), 1.0, 0.0).astype(BF)
+        acc = dot_t(wgu[:, p * part : (p + 1) * part], xu[:, :part])
+        both[...] = acc if p == 0 else both[...] + acc
+        if p + 1 < pieces:
+            relay_near(p + 1)
+        acc = dot_t(wgu[:, piece + p * part : piece + (p + 1) * part], xu[:, part : 2 * part])
+        for q in range(2, SPLIT):
+            at = q * piece + p * part
+            acc = acc + dot_t(wgu[:, at : at + part], xu[:, q * part : (q + 1) * part])
+        if p == last_tail:
+            acc = acc + dot_t(wgu[:, tail0:], xt[...])
+        both[...] = both[...] + acc
+
+    act, up = both[:slab], both[slab:]
+    hidden_t = (act / (1.0 + jnp.exp(-act)) * up).astype(BF)
+    filled = (units * UNIT_ROWS, xrows)
+    eye = jnp.where(iota(filled, 0) == iota(filled, 1), 1.0, 0.0).astype(BF)
     hidden = dot_t(eye, hidden_t).astype(BF)
     last = dot(hidden, wd[:, tail0:]).astype(BF)
 
@@ -350,9 +359,9 @@
                 halves = dot(closing, jnp.concatenate(mine, axis=0)).astype(BF).reshape(2, nodes, SUB, COL)
                 own[p, u, :, :, c * COL : (c + 1) * COL] = halves[0]
                 sib[p, u, :, :, c * COL : (c + 1) * COL] = halves[1]
+            if c == 0 and p >= 1:
+                add_core(p - 1)
         give_half(p).start()
-        if p >= 1:
-            add_core(p - 1)
         if p >= 2:
             add_chip(p - 2)
     add_core(pieces - 1)
@@ -440,15 +449,13 @@
         out_specs=hbm,
         scratch_shapes=[
             pltpu.VMEM((rows, width), BF),
-            pltpu.VMEM((slab, width), BF),
-            pltpu.VMEM((slab, width), BF),
+            pltpu.VMEM((2 * slab, width), BF),
             pltpu.VMEM((slab, width), BF),
             pltpu.VMEM((PIECES, hosted) + block, BF),
             pltpu.VMEM((PIECES, units, 2, nodes) + block, BF),
             pltpu.VMEM((xrows, SPLIT * part), BF),
             pltpu.VMEM((xrows, COL), BF),
-            pltpu.VMEM((slab, xrows), F32),
-            pltpu.VMEM((slab, xrows), F32),
+            pltpu.VMEM((2 * slab, xrows), F32),
             pltpu.VMEM((PIECES, units, nodes) + block, BF),
             pltpu.VMEM((PIECES, units, nodes) + block, BF),
             pltpu.VMEM((PIECES, units, nodes) + block, BF),

time: 75.6 us -> 76.2 us (level)
  no operation moved by 1% of the time
where the time goes in v4:
time: 76.2 us; the launch traced here: 76 us
  Pallas kernels  73.1 us (96%)
  local copies, waits for them, and re-layouts  2.85 us (4%)
    pallas_call x1, Pallas kernels, on_device(): pl.pallas_call(functools.partial(kernel, (nodes, locs)), out_shape=jax.Sh...  73.1 us
    unnamed x1, local copies, waits for them, and re-layouts  2.85 us

profile of v4, /device:TPU:24, one launch (start us, length us, event | category | flops | bytes accessed | tf_op | source)
XLA Modules:
  0.0 76.0 jit_solution(5919485600282511858)
XLA Ops:
  0.0 73.1 %shard_map.73 = bf16[128,7168]{1,0:T(8,128)(2,1)} custom-call(bf16[128,7168]{1,0:T(8,128)(2,1)} %tok_hbm.1, s32[8,128]{1,0:T(8,128)} %bitcast.12, bf16[8,128]{1,0:T(8,128)(2,1)} %bitcast.13, s32[384]{0:T(512)} %limits_ref.1, bf16[448,7168]{1,0:T(8,128)(2,1)} %bitcast.9, bf16[448,7168]{1,0:T(8,128)(2,1)} %bitcast.10, bf16[448,7168]{1,0:T(8,128)(2,1)} %bitcast.11), custom_call_target="tpu_custom_call" | custom-call | flops 3082813440 | bytes 19267584 | tf_op jit(solution)/shard_map/pallas_call | solution.py:445
  73.1 2.8 %copy.9 = bf16[128,7168]{1,0:T(8,128)(2,1)} copy(bf16[128,7168]{1,0:T(8,128)(2,1)} %shard_map.73) | data formatting | bytes 3670016

commit v5 on v4

--- a/solution.py
+++ b/solution.py
@@ -140,6 +140,22 @@
             recv_sem=recv_x.at[p, unit, node], device_id=(n, 2 * to_unit + core), device_id_type=MESH,
         )
 
+    def send_piece(p):
+        def send_out(i, _):
+            e, n, to_unit, mine = target(i)
+
+            @pl.when(mine)
+            def _():
+                pltpu.make_async_copy(pack.at[p, e], x.at[p, unit, core, node], recv_x.at[p, unit, node]).start()
+
+            @pl.when(jnp.logical_not(mine))
+            def _():
+                dispatch(p, e, n, to_unit).start()
+
+            return 0
+
+        lax.fori_loop(0, hosted, send_out, 0)
+
     for p in range(pieces):
         for c in range(cols):
             j = p * cols + c
@@ -151,21 +167,7 @@
             pack[p, :, :, c * COL : (c + 1) * COL] = acc.astype(BF).reshape(hosted, SUB, COL)
         if p == 0:
             pl.semaphore_wait(barrier, nodes * units)
-
-        def send_out(i, _):
-            e, n, to_unit, mine = target(i)
-
-            @pl.when(mine)
-            def _():
-                pltpu.make_async_copy(pack.at[p, e], x.at[p, unit, core, node], recv_x.at[p, unit, node]).start()
-
-            @pl.when(jnp.logical_not(mine))
-            def _():
-                dispatch(p, e, n, to_unit).start()
-
-            return 0
-
-        lax.fori_loop(0, hosted, send_out, 0)
+            send_piece(0)
 
     def opener(parts):
         i, m = iota((UNIT_ROWS, chunk), 0), iota((UNIT_ROWS, chunk), 1)
@@ -237,6 +239,8 @@
             return 0
 
         lax.fori_loop(0, units, first, 0)
+        if p + 1 < pieces:
+            send_piece(p + 1)
 
     def relay_far(p):
         def second(k, _):

time: 76.2 us -> 71.2 us (0.934)
  Pallas kernels: 73.1 us -> 68.1 us
    pallas_call x1, Pallas kernels: 73.1 us -> 68.1 us  [on_device(): pl.pallas_call(functools.partial(kernel, (nodes, locs)), out_shape=jax.Sh...]
where the time goes in v5:
time: 71.2 us; the launch traced here: 71 us
  Pallas kernels  68.1 us (96%)
  local copies, waits for them, and re-layouts  2.85 us (4%)
    pallas_call x1, Pallas kernels, on_device(): pl.pallas_call(functools.partial(kernel, (nodes, locs)), out_shape=jax.Sh...  68.1 us
    unnamed x1, local copies, waits for them, and re-layouts  2.85 us

profile of v5, /device:TPU:24, one launch (start us, length us, event | category | flops | bytes accessed | tf_op | source)
XLA Modules:
  0.0 71.0 jit_solution(9902353668604867621)
XLA Ops:
  0.0 68.1 %shard_map.73 = bf16[128,7168]{1,0:T(8,128)(2,1)} custom-call(bf16[128,7168]{1,0:T(8,128)(2,1)} %tok_hbm.1, s32[8,128]{1,0:T(8,128)} %bitcast.12, bf16[8,128]{1,0:T(8,128)(2,1)} %bitcast.13, s32[384]{0:T(512)} %limits_ref.1, bf16[448,7168]{1,0:T(8,128)(2,1)} %bitcast.9, bf16[448,7168]{1,0:T(8,128)(2,1)} %bitcast.10, bf16[448,7168]{1,0:T(8,128)(2,1)} %bitcast.11), custom_call_target="tpu_custom_call" | custom-call | flops 3082813440 | bytes 19267584 | tf_op jit(solution)/shard_map/pallas_call | solution.py:449
  68.2 2.8 %copy.9 = bf16[128,7168]{1,0:T(8,128)(2,1)} copy(bf16[128,7168]{1,0:T(8,128)(2,1)} %shard_map.73) | data formatting | bytes 3670016
